TPU v7x, 1024 devices: a whole 8x8x8 slice. The times are simulated.
1024 devices in a mesh: mem: 4 (over y_lo, core), lat: 8 (over x), lon: 32 (over z, y_hi).
Axes of the slice: x: 8, y: 8 (y_hi: 4, y_lo: 2; y = y_hi * 2 + y_lo), z: 8, core: 2. Of those that a mesh axis runs over, the one named last changes fastest.
Arguments:
- perturbations: bfloat16 [8, 4, 768, 1536], P('mem', None, 'lat', 'lon'), may hold values from -2 to 2
- innovation: float32 [8, 65536], P('lat', 'lon'), may hold values from -4.2 to 4.2
- obs_weight: float32 [8, 65536], P('lat', 'lon'), may hold values from 0.5 to 6, as said below
- obs_cell: int32 [8, 65536], P('lat', 'lon'), may hold values from 0 to 4607
- obs_level: int32 [8, 65536], P('lat', 'lon'), may hold values from 0 to 3
- cutoff: int32 [4], replicated, may hold values from 16 to 127
Outputs:
- solution: float32 [8, 4, 768, 512], P('mem', None, ('lat', 'lon'))
- residual: float32 [8, 4, 768, 512], P('mem', None, ('lat', 'lon'))
Inputs may be any that keep to these rules, and one draw needn't show every extreme that they name: `obs_weight`: positive weights.
All inputs are finite; a program needn't handle non-finite values.
Results may differ from a plain program's by a relative error of at most 0.0008.
Values may be sent and summed in bfloat16 or wider, within the bound.
A program may use at most 32 MiB of HBM per device.

v0:
```python
import jax
import jax.numpy as jnp
from jax import lax
from jax.sharding import Mesh
from jax.sharding import PartitionSpec as P

NLON = 1536
KMAX = 256
ITERS = 2
MEM = ("mem_0", "mem_1")
MEM_LAT_LON = ("mem_0", "mem_1", "lat", "lon_0", "lon_1")
LON = ("lon_0", "lon_1")
LAT_LON = ("lat", "lon_0", "lon_1")


def from_everyone(array, axis):
    copies = jnp.broadcast_to(array, (lax.axis_size(axis), *array.shape))
    return lax.all_to_all(copies, axis, split_axis=0, concat_axis=0, tiled=True)


def taken_together(array, axis):
    everything = from_everyone(array, axis)
    return jnp.sum(everything, axis=0)


def one_axis_at_a_time(array, axes):
    for axis in axes:
        array = lax.psum(array, axis)
    return array


def split_up(array, dim, peers):
    lengths = array.shape
    pieces = array.reshape(*lengths[:dim], peers, lengths[dim] // peers, *lengths[dim + 1 :])
    return jnp.moveaxis(pieces, dim, 0)


def in_order(pieces, dim):
    lengths = list(pieces.shape[1:])
    lengths[dim] *= pieces.shape[0]
    return jnp.moveaxis(pieces, 0, dim).reshape(lengths)


def turned_blocks(pieces, axes, order):
    inside = pieces.shape[1:]
    whole = pieces.reshape(*(lax.axis_size(a) for a in axes), *inside)
    for k in order:
        whole = lax.all_to_all(whole, axes[k], k, k, tiled=True)
    return whole.reshape(-1, *inside)


def one_axis_at_a_time_2(array, axes, order, split_dim, concat_dim):
    pieces = split_up(array, split_dim, lax.axis_size(axes))
    return in_order(turned_blocks(pieces, axes, order), concat_dim)


def basis_table(transposed):
    factor = 2.0 * jnp.pi / NLON
    if transposed:
        columns = jnp.arange(NLON, dtype=jnp.int32)[None, :]
        cos_waves = jnp.arange(KMAX, dtype=jnp.int32)[:, None]
        axis_join = 0
    else:
        columns = jnp.arange(NLON, dtype=jnp.int32)[:, None]
        cos_waves = jnp.arange(KMAX, dtype=jnp.int32)[None, :]
        axis_join = 1
    cos_phase = (columns * cos_waves % NLON).astype(jnp.float32) * factor
    sin_phase = (columns * (cos_waves + 1) % NLON).astype(jnp.float32) * factor
    joined = jnp.concatenate([jnp.cos(cos_phase), jnp.sin(sin_phase)], axis=axis_join)
    return joined / jnp.sqrt(jnp.float32(KMAX))


def spectrum_of(cutoff):
    wavenumbers = jnp.concatenate(
        [jnp.arange(KMAX, dtype=jnp.float32), jnp.arange(1, KMAX + 1, dtype=jnp.float32)]
    )
    scaled = wavenumbers[None, :] / cutoff.astype(jnp.float32)[:, None]
    return 1.0 / (1.0 + scaled * scaled)


def member_total(partial_value):
    return taken_together(partial_value, MEM)


def paired_total(residual, image):
    return (
        one_axis_at_a_time(jnp.sum(residual * residual), MEM_LAT_LON),
        one_axis_at_a_time(jnp.sum(residual * image), MEM_LAT_LON),
    )


def body(perturbations, innovation, obs_weight, obs_cell, obs_level, cutoff):
    members_here, levels, tile_rows, tile_cols = perturbations.shape
    line_rows = tile_rows // lax.axis_size(LON)
    basis_rows = basis_table(False)
    basis_cols = basis_table(True)
    spectrum = spectrum_of(cutoff)
    located = (obs_level * (tile_rows * tile_cols) + obs_cell).reshape(-1)
    weights = obs_weight.reshape(-1)

    def gridded_of(weighted):
        field = jnp.zeros((levels * tile_rows * tile_cols,), jnp.float32).at[located].add(weighted)
        return field.reshape(levels, tile_rows, tile_cols)

    def synthesize(control):
        coeffs = control * spectrum[None, :, None, :]
        synthesized = jnp.dot(
            coeffs.reshape(-1, 2 * KMAX),
            basis_cols,
            precision=lax.Precision.HIGHEST,
            preferred_element_type=jnp.float32,
        )
        return synthesized.reshape(members_here, levels, line_rows, NLON)

    def analyse(products):
        summed = jnp.dot(
            products.reshape(-1, NLON),
            basis_rows,
            precision=lax.Precision.HIGHEST,
            preferred_element_type=jnp.float32,
        )
        return (
            summed.reshape(members_here, levels, line_rows, 2 * KMAX) * spectrum[None, :, None, :]
        )

    def forward_part(control):
        synthesized = synthesize(control)
        on_tiles = one_axis_at_a_time_2(synthesized, LON, (0, 1), 3, 2)
        partial_value = jnp.sum(perturbations.astype(jnp.float32) * on_tiles, axis=0)
        return member_total(partial_value)

    def adjoint_part(gridded):
        products = perturbations.astype(jnp.float32) * gridded[None]
        line_products = lax.all_to_all(products, LON, split_axis=2, concat_axis=3, tiled=True)
        return analyse(line_products)

    def hessian(direction):
        increment = forward_part(direction)
        sampled = increment.reshape(-1)[located]
        return direction + adjoint_part(gridded_of(weights * sampled))

    right_side = adjoint_part(gridded_of(weights * innovation.reshape(-1)))
    solution = jnp.zeros_like(right_side)
    residual = right_side
    image = hessian(residual)
    norm_now, product = paired_total(residual, image)
    step_size = norm_now / product
    direction = residual
    along = image
    for iteration in range(ITERS):
        solution = solution + step_size * direction
        residual = residual - step_size * along
        if iteration + 1 < ITERS:
            image = hessian(residual)
            norm_next, product = paired_total(residual, image)
            growth = norm_next / norm_now
            step_size = norm_next / (product - growth * norm_next / step_size)
            direction = residual + growth * direction
            along = image + growth * along
            norm_now = norm_next
    return (solution, residual)


def solution(mesh):
    torus = Mesh(
        mesh.devices.reshape(2, 2, mesh.shape["lat"], 8, 4),
        ("mem_0", "mem_1", "lat", "lon_0", "lon_1"),
    )
    in_specs = (
        P(MEM, None, "lat", LON),
        P("lat", LON),
        P("lat", LON),
        P("lat", LON),
        P("lat", LON),
        P(),
    )
    out_specs = (P(MEM, None, LAT_LON, None), P(MEM, None, LAT_LON, None))
    return jax.shard_map(body, mesh=torus, in_specs=in_specs, out_specs=out_specs, check_vma=False)
```

profile of v0, /device:TPU:2, one launch (start us, length us, event | category | flops | bytes accessed | tf_op | source)
XLA Modules:
  0.0 417.3 jit_solution(3763025246386701588)
XLA Ops:
  2.1 11.2 %scatter_custom_fusion = f32[18432]{0:T(1024)S(1)} fusion(s32[2048]{0:T(1024)S(1)} %bitcast.128, f32[2048]{0:T(1024)S(1)} %mul.201, f32[]{:T(128)} %constant.20.clone.1), kind=kCustom, calls=%fused_computation.76 | custom fusion | flops 2048 | bytes 73732 | tf_op jit(solution)/shard_map/scatter-add | solution.py:102
  15.8 22.8 %all-to-all-start = ((f32[32,1,1152]{2,1,0:T(1,128)}), f32[32,1,1152]{2,1,0:T(1,128)S(1)}, u32[]{:S(2)}, u32[]{:S(2)}) async-start(f32[32,1,1152]{2,1,0:T(1,128)} %reshape.191), calls=%async_computation | async-start | bytes 294912 | tf_op jit(solution)/shard_map/all_to_all | solution.py:134
  38.7 7.0 %fusion.12 = f32[1536,256]{1,0:T(8,128)} fusion(s32[256]{0:T(256)S(1)} %iota_add_fusion.1), kind=kLoop, calls=%fused_computation.20 | loop fusion | flops 3538944 | bytes 1573888 | tf_op jit(solution)/shard_map/sin | solution.py:69
  45.7 5.9 %fusion.18 = f32[256,1536]{0,1:T(8,128)S(1)} fusion(s32[256]{0:T(256)S(1)} %iota_add_fusion.1), kind=kLoop, calls=%fused_computation.26 | loop fusion | flops 3538944 | bytes 1573888 | tf_op jit(solution)/shard_map/sin | solution.py:69
  51.6 6.1 %fusion.15 = f32[256,1536]{0,1:T(8,128)S(1)} fusion(), kind=kLoop, calls=%fused_computation.23 | loop fusion | flops 3538944 | bytes 1572864 | tf_op jit(solution)/shard_map/cos | solution.py:69
  58.2 6.7 %fusion.9 = f32[1536,256]{1,0:T(8,128)} fusion(), kind=kLoop, calls=%fused_computation.17 | loop fusion | flops 3538944 | bytes 1572864 | tf_op jit(solution)/shard_map/cos | solution.py:69
  67.1 2.0 reshape.192
  70.9 1.9 dot_general.25
  72.8 3.8 fusion.34
  76.7 4.9 %fusion.53 = f32[2,4,3,32,48]{4,1,3,2,0:T(4,128)S(1)} fusion(f32[32,48,512,1,1]{2,1,0,4,3:T(8,128)S(1)} %bitcast.110, f32[2,4,3,512]{3,1,2,0:T(4,128)S(1)} %fusion.34, f32[4,512]{1,0:T(4,128)S(1)} %fusion.66), kind=kOutput, calls=%fused_computation.60 | convolution fusion | flops 226504704 | bytes 3350528 | tf_op jit(solution)/shard_map/dot_general | solution.py:107
  82.4 2.1 reshape.193
  84.5 16.3 %all_to_all.75 = f32[8,1,4608]{2,1,0:T(1,128)} all-to-all(f32[8,1,4608]{2,1,0:T(1,128)} %reshape.193), channel_id=1, replica_groups=mesh['mem_0'=2,'mem_1'=2,'lat'=8,'lon_0'=8,'lon_1'=4] {'lon_0'}, dimensions={0} | all-to-all | bytes 294912 | tf_op jit(solution)/shard_map/all_to_all | solution.py:48
  100.8 2.6 reduce.1
  103.3 2.0 reshape.194
  107.2 2.1 reshape.195
  109.3 15.6 %all_to_all.76 = f32[4,1,9216]{2,1,0:T(1,128)} all-to-all(f32[4,1,9216]{2,1,0:T(1,128)} %reshape.195), channel_id=1, replica_groups=mesh['mem_0'=2,'mem_1'=2,'lat'=8,'lon_0'=8,'lon_1'=4] {'lon_1'}, dimensions={0} | all-to-all | bytes 294912 | tf_op jit(solution)/shard_map/all_to_all | solution.py:48
  124.9 2.6 reduce.2
  127.5 2.0 reshape.196
  135.2 4.5 %all-to-all-start.3 = ((f32[4,4,96,48]{2,3,1,0:T(8,128)}), f32[4,4,96,48]{2,3,1,0:T(8,128)}, u32[]{:S(2)}, u32[]{:S(2)}) async-start(f32[4,4,96,48]{2,3,1,0:T(8,128)} %broadcast_in_dim.4), calls=%async_computation.3 | async-start | bytes 786432 | tf_op jit(solution)/shard_map/all_to_all | solution.py:18
  139.7 7.5 %all-to-all-done.3 = f32[4,4,96,48]{2,3,1,0:T(8,128)} async-done(((f32[4,4,96,48]{2,3,1,0:T(8,128)}), f32[4,4,96,48]{2,3,1,0:T(8,128)}, u32[]{:S(2)}, u32[]{:S(2)}) %all-to-all-start.3) | async-done | bytes 294944 | tf_op jit(solution)/shard_map/all_to_all | solution.py:18
  151.7 11.8 %gather_fusion = f32[2048]{0:T(1024)S(1)} fusion(f32[18432]{0:T(1024)S(1)} %reshape.136, s32[2048]{0:T(1024)S(1)} %broadcast_clamp_fusion), kind=kCustom, calls=%fused_computation | custom fusion | bytes 24576 | tf_op jit(solution)/shard_map/gather | solution.py:139
  163.5 11.2 %scatter_custom_fusion.1 = f32[18432]{0:T(1024)S(1)} fusion(s32[2048]{0:T(1024)S(1)} %bitcast.130, f32[2048]{0:T(1024)S(1)} %mul.227, f32[]{:T(128)} %constant.20.clone.1), kind=kCustom, calls=%fused_computation.74 | custom fusion | flops 2048 | bytes 73732 | tf_op jit(solution)/shard_map/scatter-add | solution.py:102
  177.4 2.1 reshape.197
  179.5 17.1 %all_to_all.77 = f32[32,1,1152]{2,1,0:T(1,128)} all-to-all(f32[32,1,1152]{2,1,0:T(1,128)} %reshape.197), channel_id=1, replica_groups=mesh['mem_0'=2,'mem_1'=2,'lat'=8,'lon_0'=8,'lon_1'=4] {'lon_0','lon_1'}, dimensions={0} | all-to-all | bytes 294912 | tf_op jit(solution)/shard_map/all_to_all | solution.py:134
  196.6 2.6 reduce.3
  199.2 2.0 reshape.198
  203.0 1.9 dot_general.30
  204.9 4.4 %multiply_reduce_fusion.2 = (f32[]{:T(128)}, f32[]{:T(128)}, f32[2,4,3,512]{3,1,2,0:T(4,128)S(1)}) fusion(f32[2,4,3,512]{3,1,2,0:T(4,128)S(1)} %fusion.34, f32[4,512]{1,0:T(4,128)S(1)} %fusion.66, f32[2,4,3,1536]{3,1,2,0:T(4,128)} %dot_general.30, f32[1536,256]{1,0:T(8,128)} %fusion.12, f32[1536,256]{1,0:T(8,128)} %fusion.9), kind=kOutput, calls=%fused_computation.68 | convolution fusion | flops 228139008 | bytes 3399688 | tf_op jit(solution)/shard_map/dot_general | solution.py:116
  209.4 5.6 %all-reduce.9 = (f32[]{:T(128)}, f32[]{:T(128)}) all-reduce(f32[]{:T(128)} %get-tuple-element.5, f32[]{:T(128)} %get-tuple-element.4), channel_id=1, replica_groups=mesh['mem_0'=2,'mem_1'=2,'lat'=8,'lon_0'=8,'lon_1'=4] {'mem_0'}, use_global_device_ids=true, to_apply=%region_2.3 | all-reduce | flops 2 | bytes 16 | tf_op jit(solution)/shard_map/psum | solution.py:28
  214.9 3.1 all-reduce.7
  218.0 16.4 %all-reduce.3 = (f32[]{:T(128)}, f32[]{:T(128)}) all-reduce(f32[]{:T(128)} %get-tuple-element.20, f32[]{:T(128)} %get-tuple-element.21), channel_id=1, replica_groups=mesh['mem_0'=2,'mem_1'=2,'lat'=8,'lon_0'=8,'lon_1'=4] {'lat'}, use_global_device_ids=true, to_apply=%region_4.5 | all-reduce | flops 2 | bytes 16 | tf_op jit(solution)/shard_map/psum | solution.py:28
  234.4 16.1 %all-reduce.1 = (f32[]{:T(128)}, f32[]{:T(128)}) all-reduce(f32[]{:T(128)} %get-tuple-element.12, f32[]{:T(128)} %get-tuple-element.13), channel_id=1, replica_groups=mesh['mem_0'=2,'mem_1'=2,'lat'=8,'lon_0'=8,'lon_1'=4] {'lon_0'}, use_global_device_ids=true, to_apply=%region_5.6 | all-reduce | flops 2 | bytes 16 | tf_op jit(solution)/shard_map/psum | solution.py:28
  250.5 10.2 %all-reduce.5 = (f32[]{:T(128)}, f32[]{:T(128)}) all-reduce(f32[]{:T(128)} %get-tuple-element.8, f32[]{:T(128)} %get-tuple-element.9), channel_id=1, replica_groups=mesh['mem_0'=2,'mem_1'=2,'lat'=8,'lon_0'=8,'lon_1'=4] {'lon_1'}, use_global_device_ids=true, to_apply=%region_6.7 | all-reduce | flops 2 | bytes 16 | tf_op jit(solution)/shard_map/psum | solution.py:28
  262.0 4.9 %fusion.51 = f32[2,4,3,32,48]{4,1,3,2,0:T(4,128)S(1)} fusion(f32[32,48,512,1,1]{2,1,0,4,3:T(8,128)S(1)} %bitcast.111, f32[2,4,3,512]{3,1,2,0:T(4,128)S(1)} %multiply_subtract_fusion.1, f32[4,512]{1,0:T(4,128)S(1)} %fusion.66), kind=kOutput, calls=%fused_computation.58 | convolution fusion | flops 226504704 | bytes 3350528 | tf_op jit(solution)/shard_map/dot_general | solution.py:107
  267.4 13.3 %all_to_all.78 = f32[8,1,4608]{2,1,0:T(1,128)S(1)} all-to-all(f32[8,1,4608]{2,1,0:T(1,128)S(1)} %reshape.199), channel_id=1, replica_groups=mesh['mem_0'=2,'mem_1'=2,'lat'=8,'lon_0'=8,'lon_1'=4] {'lon_0'}, dimensions={0} | all-to-all | bytes 294912 | tf_op jit(solution)/shard_map/all_to_all | solution.py:48
  282.6 13.3 %all_to_all.79 = f32[4,1,9216]{2,1,0:T(1,128)S(1)} all-to-all(f32[4,1,9216]{2,1,0:T(1,128)S(1)} %reshape.201), channel_id=1, replica_groups=mesh['mem_0'=2,'mem_1'=2,'lat'=8,'lon_0'=8,'lon_1'=4] {'lon_1'}, dimensions={0} | all-to-all | bytes 294912 | tf_op jit(solution)/shard_map/all_to_all | solution.py:48
  298.2 9.8 %all_to_all.80 = f32[4,4,96,48]{2,3,1,0:T(8,128)S(1)} all-to-all(f32[4,4,96,48]{2,3,1,0:T(8,128)S(1)} %broadcast_in_dim.5), channel_id=1, replica_groups=mesh['mem_0'=2,'mem_1'=2,'lat'=8,'lon_0'=8,'lon_1'=4] {'mem_0','mem_1'}, dimensions={0} | all-to-all | bytes 589824 | tf_op jit(solution)/shard_map/all_to_all | solution.py:18
  308.3 11.8 %gather_fusion.1 = f32[2048]{0:T(1024)S(1)} fusion(f32[18432]{0:T(1024)S(1)} %reshape.140, s32[2048]{0:T(1024)S(1)} %broadcast_clamp_fusion), kind=kCustom, calls=%fused_computation.1 | custom fusion | bytes 24576 | tf_op jit(solution)/shard_map/gather | solution.py:139
  320.1 11.2 %scatter_custom_fusion.2 = f32[18432]{0:T(1024)S(1)} fusion(s32[2048]{0:T(1024)S(1)} %bitcast.131, f32[2048]{0:T(1024)S(1)} %mul.239, f32[]{:T(128)} %constant.20.clone.1), kind=kCustom, calls=%fused_computation.72 | custom fusion | flops 2048 | bytes 73732 | tf_op jit(solution)/shard_map/scatter-add | solution.py:102
  332.5 2.2 reshape.203
  334.7 16.3 %all_to_all.81 = f32[32,1,1152]{2,1,0:T(1,128)S(1)} all-to-all(f32[32,1,1152]{2,1,0:T(1,128)} %reshape.203), channel_id=1, replica_groups=mesh['mem_0'=2,'mem_1'=2,'lat'=8,'lon_0'=8,'lon_1'=4] {'lon_0','lon_1'}, dimensions={0} | all-to-all | bytes 294912 | tf_op jit(solution)/shard_map/all_to_all | solution.py:134
  352.6 2.0 reshape.204
  357.7 2.5 multiply_reduce_fusion
  360.2 5.6 %all-reduce.8 = (f32[]{:T(128)}, f32[]{:T(128)}) all-reduce(f32[]{:T(128)} %get-tuple-element.3, f32[]{:T(128)} %get-tuple-element.2), channel_id=1, replica_groups=mesh['mem_0'=2,'mem_1'=2,'lat'=8,'lon_0'=8,'lon_1'=4] {'mem_0'}, use_global_device_ids=true, to_apply=%region_17.18 | all-reduce | flops 2 | bytes 16 | tf_op jit(solution)/shard_map/psum | solution.py:28
  365.8 3.1 all-reduce.6
  368.9 16.6 %all-reduce.2 = (f32[]{:T(128)}, f32[]{:T(128)}) all-reduce(f32[]{:T(128)} %get-tuple-element.18, f32[]{:T(128)} %get-tuple-element.19), channel_id=1, replica_groups=mesh['mem_0'=2,'mem_1'=2,'lat'=8,'lon_0'=8,'lon_1'=4] {'lat'}, use_global_device_ids=true, to_apply=%region_19.20 | all-reduce | flops 2 | bytes 16 | tf_op jit(solution)/shard_map/psum | solution.py:28
  385.5 16.0 %all-reduce = (f32[]{:T(128)}, f32[]{:T(128)}) all-reduce(f32[]{:T(128)} %get-tuple-element.10, f32[]{:T(128)} %get-tuple-element.11), channel_id=1, replica_groups=mesh['mem_0'=2,'mem_1'=2,'lat'=8,'lon_0'=8,'lon_1'=4] {'lon_0'}, use_global_device_ids=true, to_apply=%region_20.21 | all-reduce | flops 2 | bytes 16 | tf_op jit(solution)/shard_map/psum | solution.py:28
  401.5 10.2 %all-reduce.4 = (f32[]{:T(128)}, f32[]{:T(128)}) all-reduce(f32[]{:T(128)} %get-tuple-element.6, f32[]{:T(128)} %get-tuple-element.7), channel_id=1, replica_groups=mesh['mem_0'=2,'mem_1'=2,'lat'=8,'lon_0'=8,'lon_1'=4] {'lon_1'}, use_global_device_ids=true, to_apply=%region_21.22 | all-reduce | flops 2 | bytes 16 | tf_op jit(solution)/shard_map/psum | solution.py:28
  (67 shorter events, 37.0 us)
Async XLA Ops:
  15.8 49.1 %all-to-all-start = ((f32[32,1,1152]{2,1,0:T(1,128)}), f32[32,1,1152]{2,1,0:T(1,128)S(1)}, u32[]{:S(2)}, u32[]{:S(2)}) async-start(f32[32,1,1152]{2,1,0:T(1,128)} %reshape.191), calls=%async_computation | async-start | bytes 294912 | tf_op jit(solution)/shard_map/all_to_all | solution.py:134
  45.7 12.0 %copy-start.3 = (s32[4]{0:T(128)S(1)}, s32[4]{0:T(128)}, u32[]{:S(2)}) copy-start(s32[4]{0:T(128)} %param.11) | copy-start | bytes 52
  135.2 12.0 %all-to-all-start.3 = ((f32[4,4,96,48]{2,3,1,0:T(8,128)}), f32[4,4,96,48]{2,3,1,0:T(8,128)}, u32[]{:S(2)}, u32[]{:S(2)}) async-start(f32[4,4,96,48]{2,3,1,0:T(8,128)} %broadcast_in_dim.4), calls=%async_computation.3 | async-start | bytes 786432 | tf_op jit(solution)/shard_map/all_to_all | solution.py:18
  151.6 11.8 %copy-start.2 = (f32[1,2048]{1,0:T(1,128)S(1)}, f32[1,2048]{1,0:T(1,128)}, u32[]{:S(2)}) copy-start(f32[1,2048]{1,0:T(1,128)} %param.8) | copy-start | bytes 24580
  331.6 26.1 %copy-start.1 = (f32[1536,256]{1,0:T(8,128)S(1)}, f32[1536,256]{1,0:T(8,128)}, u32[]{:S(2)}) copy-start(f32[1536,256]{1,0:T(8,128)} %fusion.9) | copy-start | bytes 4718596
  332.4 25.3 %copy-start = (f32[1536,256]{1,0:T(8,128)S(1)}, f32[1536,256]{1,0:T(8,128)}, u32[]{:S(2)}) copy-start(f32[1536,256]{1,0:T(8,128)} %fusion.12) | copy-start | bytes 4718596
where the time goes:
time: 422 us; the launch traced here: 417 us
  blocking collectives  205 us (49%)
  other arithmetic  79.6 us (19%)
  local copies, waits for them, and re-layouts  70.4 us (17%)
  starting transfers between devices  27.3 us (6%)
  matrix products  20.6 us (5%)
  waiting for transfers between devices  7.49 us (2%)
  between operations  7.27 us (2%)
    psum x10, blocking collectives, one_axis_at_a_time(): array = lax.psum(array, axis)  103 us
    all_to_all x4, blocking collectives, turned_blocks(): whole = lax.all_to_all(whole, axes[k], k, k, tiled=True)  58.5 us
    scatter-add x3, other arithmetic, gridded_of(): jnp.zeros((levels * tile_rows * tile_cols,), jnp.float32).at[located]  33.7 us
    all_to_all x2, blocking collectives, adjoint_part(): lax.all_to_all(products, LON, split_axis=2, concat_axis=3, tiled=True)  33.5 us
    unnamed x25, local copies, waits for them, and re-layouts  24.2 us
    gather x2, local copies, waits for them, and re-layouts, hessian(): sampled = increment.reshape(-1)[located]  23.6 us
    all_to_all x1, starting transfers between devices, adjoint_part(): lax.all_to_all(products, LON, split_axis=2, concat_axis=3, tiled=True)  22.8 us
    sin x2, other arithmetic, basis_table(): jnp.sin(sin_phase)  12.9 us
  transfers between devices with their start and end apart: 2, of which 1 were waited for; matrix products, arithmetic and copies ran while one was open for 6% of the time, Pallas kernels for 0%

commit v1 on v0

v1 whole, which is shorter than its diff:
```python
import jax
import jax.numpy as jnp
import ml_dtypes
import numpy as np
from jax import lax
from jax.experimental import pallas as pl
from jax.experimental.pallas import tpu as pltpu
from jax.sharding import PartitionSpec as P

MESH = pl.DeviceIdType.MESH
BF16 = jnp.bfloat16
F32 = jnp.float32
NLON = 1536
KMAX = 256
MEMBERS = 8
N_MEM = 4
N_LAT = 8
N_LON = 32
ROWS = 96
COLS = 48
LINES = 3
QUARTER = NLON // 4
SLOT = 16


def halves(table):
    high = table.astype(ml_dtypes.bfloat16)
    low = (table - high.astype(np.float64)).astype(ml_dtypes.bfloat16)
    return np.stack([high, low])


def constants():
    piece, source, i = np.meshgrid(np.arange(3), np.arange(8), np.arange(16), indexing="ij")
    column = (48 * source + 16 * piece + i).reshape(-1)

    def table(columns, cosines, sines):
        angle = 2.0 * np.pi / NLON
        cos = np.cos((columns[:, None] * cosines[None] % NLON) * angle)
        sin = np.sin((columns[:, None] * sines[None] % NLON) * angle)
        return np.concatenate([cos, sin], axis=1) / 16.0

    c0, s0 = np.arange(0, 256, 4), np.arange(4, 257, 4)
    c2 = np.arange(2, 256, 4)
    c1 = np.arange(1, 256, 2)
    t0 = table(column, c0, s0)
    t2 = table(column, c2, c2)
    t1 = table(np.concatenate([column, QUARTER + column]), c1, c1)
    wave = np.concatenate([c0, s0, c2, c2, c1, c1])
    natural = np.concatenate([c0, 255 + s0, c2, 255 + c2, c1, 255 + c1])
    order = np.zeros((512, 512))
    order[np.arange(512), natural] = 1

    pack = np.zeros((5, N_LON * SLOT, ROWS))
    unpack = np.zeros((216, 128))
    for s in range(LINES):
        for u in range(5):
            peer = np.arange(N_LON)
            pack[u, peer * SLOT + 3 * u + s, 3 * peer + s] = 1
        for piece in range(3):
            for m in range(MEMBERS):
                row = piece * 24 + s * 8 + m
                unpack[row, m * SLOT + piece * 3 + s] = 1
                for f in range(2):
                    for h in range(2):
                        r = (9, 12, 9)[piece] + s
                        q = (0, 0, 4)[piece] + 2 * f + h
                        unpack[72 * (f + 1) + row, q * SLOT + r] = 1
    small = [a.astype(ml_dtypes.bfloat16) for a in (pack, unpack)]
    tables = [halves(t) for t in (t0, t2, t1, t0.T, t2.T, t1.T)]
    return small + tables + [order.astype(ml_dtypes.bfloat16), np.broadcast_to(wave, (8, 512)).astype(np.float32)]


def dot(a, b):
    return jnp.dot(a, b, preferred_element_type=F32)


def dot_nt(a, b):
    return lax.dot_general(a, b, (((1,), (1,)), ((), ())), preferred_element_type=F32)


def split(x):
    high = x.astype(BF16)
    return high, (x - high.astype(F32)).astype(BF16)


def dot3(x, table):
    high, low = split(x)
    both = dot(jnp.concatenate([high, low], axis=0), table[0])
    n = x.shape[0]
    return both[:n] + (both[n:] + dot(high, table[1]))


def kernel(p_ref, inn_in, wt_in, cell_in, lev_in, cut_ref, *refs):
    n_const = 10
    loads_in = (inn_in, wt_in, cell_in, lev_in) + refs[:n_const]
    sol_ref, res_ref = refs[n_const : n_const + 2]
    scratch = refs[n_const + 2 :]
    n_load = n_const + 4
    loads_ref = scratch[:n_load]
    (mine, packed, got, x_ref, g_ref, n_ref, c_ref, out_c, in_c, part1, sums1, part2, sums2, last) = scratch[n_load : n_load + 14]
    load_sem, send_a, recv_a, send_b, recv_b, send_c, recv_c, send_s, recv_s = scratch[n_load + 14 :]
    inn_ref, wt_ref, cell_ref, lev_ref, pack, unpack, t0, t2, t1, b0, b2, b1, order, wave = loads_ref

    mem, lat, lon = lax.axis_index("mem"), lax.axis_index("lat"), lax.axis_index("lon")
    group = mem * N_LAT + lat

    def lon_peer(d):
        return {"mem": mem, "lat": lat, "lon": lax.rem(lon + d, N_LON)}

    def group_peer(d):
        other = lax.rem(group + d, N_MEM * N_LAT)
        return {"mem": other // N_LAT, "lat": lax.rem(other, N_LAT), "lon": lon}

    def mem_peer(d):
        return {"mem": lax.rem(mem + d, N_MEM), "lat": lat, "lon": lon}

    barrier = pltpu.get_barrier_semaphore()

    @pl.loop(1, 32)
    def _(d):
        pl.semaphore_signal(barrier, inc=1, device_id=group_peer(d), device_id_type=MESH)
        pl.semaphore_signal(barrier, inc=1, device_id=lon_peer(d), device_id_type=MESH)

    loads = [pltpu.make_async_copy(loads_in[k], loads_ref[k], load_sem.at[k]) for k in range(n_load)]
    for copy in loads:
        copy.start()
    own_members = pltpu.make_async_copy(p_ref.at[:, mem], mine.at[mem], load_sem.at[n_load])
    own_members.start()

    out_c[...] = jnp.zeros_like(out_c)

    for k in range(4):
        loads[k].wait()
    cell = cell_ref[...].astype(F32)
    row_of = jnp.floor((cell + 0.5) * (1.0 / COLS))
    col_of = cell - COLS * row_of
    key = row_of + ROWS * lev_ref[...].astype(F32)
    rows = lax.broadcasted_iota(jnp.int32, (ROWS, 1), 0) + ROWS * mem
    row_hot = jnp.where(rows.astype(F32) == key, 1.0, 0.0).astype(BF16)
    weight = wt_ref[...]
    col_hit = lax.broadcasted_iota(jnp.int32, (COLS, 1), 0).astype(F32) == col_of
    tile = jnp.zeros((2 * COLS, ROWS), F32)
    parts = [split(weight * inn_ref[...]), split(weight)]
    for h in range(2):
        placed = jnp.concatenate([jnp.where(col_hit, part[h].astype(F32), 0.0) for part in parts], axis=0).astype(BF16)
        tile += dot_nt(placed, row_hot)
    tiles = split(tile)

    def of_fields(piece):
        return [tiles[h][f * COLS + piece * 16 : f * COLS + piece * 16 + 16] for f in range(2) for h in range(2)]

    nothing = jnp.zeros((64, ROWS), BF16)
    chunks = [jnp.concatenate(of_fields(0) + of_fields(2), axis=0), jnp.concatenate(of_fields(1) + [nothing], axis=0)]
    loads[4].wait()
    message = dot_nt(pack[3], chunks[0]) + dot_nt(pack[4], chunks[1])

    pl.semaphore_wait(barrier, 62)

    for d in (2, 3, 1):
        peer = mem_peer(d)
        pltpu.make_async_remote_copy(
            p_ref.at[:, peer["mem"]], mine.at[mem], send_a, recv_a, device_id=peer, device_id_type=MESH
        ).start()
    own_members.wait()
    three = mine.at[pl.ds(0, 3)]
    pltpu.make_async_copy(three, three, recv_a).wait()
    for piece in range(3):
        chunk = [mine[k, a, piece * 16 : piece * 16 + 16, :] for k in range(N_MEM) for a in range(2)]
        message += dot_nt(pack[piece], jnp.concatenate(chunk, axis=0))
    packed[...] = message.astype(BF16).reshape(N_LON, SLOT, 128)

    @pl.loop(1, 32)
    def _(d):
        peer = lon_peer(d)
        pltpu.make_async_remote_copy(
            packed.at[peer["lon"]], got.at[lon], send_b, recv_b, device_id=peer, device_id_type=MESH
        ).start()

    got[lon] = packed[lon]
    for copy in loads[5:]:
        copy.wait()
    cutoff = cut_ref[mem].astype(F32)
    scaled = wave[0:1, :] / cutoff
    spectrum = 1.0 / (1.0 + scaled * scaled)
    lots = got.at[pl.ds(0, 31)]
    pltpu.make_async_copy(lots, lots, recv_b).wait()

    lane = lax.broadcasted_iota(jnp.int32, (SLOT, 128), 1)
    for quarter in range(4):
        blocks = [got[8 * quarter + k].astype(F32) for k in range(8)]
        for bit in range(3):
            width = 16 << bit
            low_side = (lane & width) == 0
            for k in range(8):
                if not k & (1 << bit):
                    a, b = blocks[k], blocks[k | (1 << bit)]
                    blocks[k] = jnp.where(low_side, a, pltpu.roll(b, width, 1))
                    blocks[k | (1 << bit)] = jnp.where(low_side, pltpu.roll(a, 128 - width, 1), b)
        stack = jnp.concatenate(blocks, axis=0).astype(BF16)
        straight = dot(unpack[...], stack)
        for piece in range(3):
            at = (3 * quarter + piece) * 128
            for f, ref in enumerate((x_ref, g_ref, n_ref)):
                row = 72 * f + 24 * piece
                ref[:, at : at + 128] = straight[row : row + 24]

    def quarters(x):
        return [x[:, k * QUARTER : (k + 1) * QUARTER] for k in range(4)]

    def analyse(field):
        q0, q1, q2, q3 = quarters(x_ref[...] * field)
        even, odd = q0 + q2, q1 + q3
        found = [
            dot3(even + odd, t0),
            dot3(even - odd, t2),
            dot3(jnp.concatenate([q0 - q2, q1 - q3], axis=1), t1),
        ]
        return jnp.concatenate(found, axis=1) * spectrum

    def synthesize(coeffs):
        scaled = coeffs * spectrum
        e0 = dot3(scaled[:, :128], b0)
        e2 = dot3(scaled[:, 128:256], b2)
        o = dot3(scaled[:, 256:], b1)
        oa, ob = o[:, :QUARTER], o[:, QUARTER:]
        plus, minus = e0 + e2, e0 - e2
        line = jnp.concatenate([plus + oa, minus + ob, plus - oa, minus - ob], axis=1)
        seen = (x_ref[...] * line).reshape(LINES, MEMBERS, NLON)
        total = jnp.sum(seen, axis=1, keepdims=True)
        return jnp.broadcast_to(total, (LINES, MEMBERS, NLON)).reshape(LINES * MEMBERS, NLON)

    def send_coeffs(v, coeffs):
        c_ref[...] = coeffs
        for k in range(N_MEM):
            for m in range(2):
                for s in range(LINES):
                    out_c[v, k, m * LINES + s : m * LINES + s + 1, :] = c_ref[s * 8 + 2 * k + m : s * 8 + 2 * k + m + 1, :]
        for d in (2, 3, 1):
            peer = mem_peer(d)
            pltpu.make_async_remote_copy(
                out_c.at[v, peer["mem"]], in_c.at[v, mem], send_c.at[v], recv_c.at[v], device_id=peer, device_id_type=MESH
            ).start()
        in_c[v, mem] = out_c[v, mem]

    def total_of(x):
        return jnp.sum(x, keepdims=True)

    f0 = g_ref[...]
    coeffs = analyse(f0)
    send_coeffs(0, coeffs)
    u0 = synthesize(coeffs)
    f1 = n_ref[...] * u0
    m1, m2 = total_of(f0 * u0), total_of(f1 * u0)
    coeffs = analyse(f1)
    send_coeffs(1, coeffs)
    u1 = synthesize(coeffs)
    f2 = n_ref[...] * u1
    m3, m4 = total_of(f1 * u1), total_of(f2 * u1)

    place = lax.broadcasted_iota(jnp.int32, (1, 128), 1)
    own = jnp.zeros((1, 128), F32)
    for k, value in enumerate((m1, m2, m3, m4)):
        own = jnp.where(place == k, value, own)

    def send_sums(stage, part, sums, peer_of, index):
        @pl.loop(1, 32)
        def _(d):
            pltpu.make_async_remote_copy(
                part, sums.at[index], send_s.at[stage], recv_s.at[stage], device_id=peer_of(d), device_id_type=MESH
            ).start()

    def wait_sums(stage, sums):
        lots = sums.at[pl.ds(0, 31)]
        pltpu.make_async_copy(lots, lots, recv_s.at[stage]).wait()
        return jnp.sum(sums[...], axis=0)

    part1[...] = own
    send_sums(0, part1, sums1, lon_peer, lon)
    sums1[lon] = own
    send_coeffs(2, analyse(f2))
    own = wait_sums(0, sums1)
    part2[...] = own
    send_sums(1, part2, sums2, group_peer, group)
    sums2[group] = own
    three = in_c.at[0, pl.ds(0, 3)]
    for v in range(3):
        pltpu.make_async_copy(three, three, recv_c.at[v]).wait()
    v0, v1, v2 = (in_c[v].reshape(32, 512) for v in range(3))
    moments = wait_sums(1, sums2)
    m1, m2, m3, m4 = (total_of(jnp.where(place == k, moments, 0.0)) for k in range(4))

    step = m1 / (m1 + m2)
    rest = 1.0 - step
    norm = rest * rest * m1 - 2.0 * step * rest * m2 + step * step * m3
    growth = norm / m1
    a = rest + growth
    curved = a * a * (m1 + m2) - 2.0 * a * step * (m2 + m3) + step * step * (m3 + m4)
    step_next = norm / curved
    found = (step + step_next * a) * v0 - (step_next * step) * v1
    left = (rest - step_next * a) * v0 - (step + step_next * (a - step)) * v1 + (step_next * step) * v2
    high, low = split(jnp.concatenate([found, left], axis=0))
    both = dot(jnp.concatenate([high, low], axis=0), order[...])
    last[...] = (both[:64] + both[64:]).reshape(8, 8, 512)
    for m in range(2):
        for s in range(LINES):
            for k in range(N_MEM):
                row = LINES * m + s
                sol_ref[m, s, k : k + 1, :] = last[k, row : row + 1, :]
                res_ref[m, s, k : k + 1, :] = last[N_MEM + k, row : row + 1, :]

    three = mine.at[pl.ds(0, 3)]
    pltpu.make_async_copy(three, three, send_a).wait()
    lots = got.at[pl.ds(0, 31)]
    pltpu.make_async_copy(lots, lots, send_b).wait()
    three = in_c.at[0, pl.ds(0, 3)]
    for v in range(3):
        pltpu.make_async_copy(three, three, send_c.at[v]).wait()
    for stage, sums in enumerate((sums1, sums2)):
        lots = sums.at[pl.ds(0, 31)]
        pltpu.make_async_copy(lots, lots, send_s.at[stage]).wait()


def body(perturbations, innovation, obs_weight, obs_cell, obs_level, cutoff):
    consts = [jnp.asarray(c) for c in constants()]
    vmem = pl.BlockSpec(memory_space=pltpu.VMEM)
    anywhere = pl.BlockSpec(memory_space=pl.ANY)
    out = jax.ShapeDtypeStruct((2, LINES, N_MEM, 2 * KMAX), F32)
    dma = pltpu.SemaphoreType.DMA
    obs = (innovation, obs_weight, obs_cell, obs_level)
    scratch = [pltpu.VMEM(c.shape, c.dtype) for c in (*obs, *consts)] + [
        pltpu.VMEM((N_MEM, 2, COLS, ROWS), BF16),
        pltpu.VMEM((N_LON, SLOT, 128), BF16),
        pltpu.VMEM((N_LON, SLOT, 128), BF16),
        pltpu.VMEM((24, NLON), F32),
        pltpu.VMEM((24, NLON), F32),
        pltpu.VMEM((24, NLON), F32),
        pltpu.VMEM((24, 512), F32),
        pltpu.VMEM((3, 4, 8, 512), F32),
        pltpu.VMEM((3, 4, 8, 512), F32),
        pltpu.VMEM((1, 128), F32),
        pltpu.VMEM((32, 1, 128), F32),
        pltpu.VMEM((1, 128), F32),
        pltpu.VMEM((32, 1, 128), F32),
        pltpu.VMEM((8, 8, 512), F32),
        dma((len(obs) + len(consts) + 1,)),
        dma,
        dma,
        dma,
        dma,
        dma((3,)),
        dma((3,)),
        dma((2,)),
        dma((2,)),
    ]
    found, left = pl.pallas_call(
        kernel,
        out_shape=(out, out),
        in_specs=[anywhere] * 5 + [pl.BlockSpec(memory_space=pltpu.SMEM)] + [anywhere] * len(consts),
        out_specs=(vmem, vmem),
        scratch_shapes=scratch,
        compiler_params=pltpu.CompilerParams(
            collective_id=0, has_side_effects=True, vmem_limit_bytes=62 * 1024 * 1024
        ),
    )(jnp.swapaxes(perturbations, 2, 3), *obs, cutoff, *consts)
    return jnp.swapaxes(found, 1, 2), jnp.swapaxes(left, 1, 2)


def solution(mesh):
    in_specs = (
        P("mem", None, "lat", "lon"),
        P("lat", "lon"),
        P("lat", "lon"),
        P("lat", "lon"),
        P("lat", "lon"),
        P(),
    )
    out_specs = (P("mem", None, ("lat", "lon"), None), P("mem", None, ("lat", "lon"), None))
    return jax.shard_map(body, mesh=mesh, in_specs=in_specs, out_specs=out_specs, check_vma=False)
```

time: 422 us -> 56.6 us (0.13)
  the two profiles are of different devices: /device:TPU:2 before, /device:TPU:1 now
where the time goes in v1:
time: 56.6 us; the launch traced here: 56.4 us
  Pallas kernels  53.6 us (95%)
  local copies, waits for them, and re-layouts  2.06 us (4%)
  between operations  0.65 us (1%)
    pallas_call x1, Pallas kernels, body(): pl.pallas_call(kernel, out_shape=(out, out), in_specs=[anywhere] * 5 + [p...  53.6 us
    unnamed x4, local copies, waits for them, and re-layouts  2.06 us

profile of v1, /device:TPU:1, one launch (start us, length us, event | category | flops | bytes accessed | tf_op | source)
XLA Modules:
  0.0 56.4 jit_solution(11242133212848790921)
XLA Ops:
  0.6 53.6 %shard_map.167 = (f32[2,3,4,512]{3,2,1,0:T(4,128)}, f32[2,3,4,512]{3,2,1,0:T(4,128)}) custom-call(bf16[2,4,48,96]{3,2,1,0:T(8,128)(2,1)} %bitcast.3, f32[1,2048]{1,0:T(1,128)} %inn_in.1, f32[1,2048]{1,0:T(1,128)} %wt_in.1, s32[1,2048]{1,0:T(1,128)} %cell_in.1, s32[1,2048]{1,0:T(1,128)} %lev_in.1, s32[4]{0:T(128)} %cut_ref.1, ...), custom_call_target="tpu_custom_call" | custom-call | tf_op jit(solution)/shard_map/pallas_call | solution.py:355
  54.3 0.0 copy-start
  54.3 1.4 %copy.20 = f32[2,4,3,512]{3,1,2,0:T(4,128)} copy(f32[2,4,3,512]{3,1,2,0:T(4,128)} %bitcast.5) | data formatting | bytes 98304
  55.7 0.0 copy-done
  55.7 0.6 %copy.21 = f32[2,4,3,512]{3,1,2,0:T(4,128)} copy(f32[2,4,3,512]{3,1,2,0:T(4,128)S(1)} %bitcast.4) | data formatting | bytes 98304
Async XLA Ops:
  54.3 1.4 %copy-start = (f32[2,3,4,512]{3,2,1,0:T(4,128)S(1)}, f32[2,3,4,512]{3,2,1,0:T(4,128)}, u32[]{:S(2)}) copy-start(f32[2,3,4,512]{3,2,1,0:T(4,128)} %get-tuple-element.5) | copy-start | bytes 147460

commit v2 on v1

--- a/solution.py
+++ b/solution.py
@@ -21,6 +21,15 @@
 LINES = 3
 QUARTER = NLON // 4
 SLOT = 16
+
+
+def farthest_first(first, second, hops):
+    steps = [(i, j) for i in range(first) for j in range(second) if i or j]
+    return sorted(steps, key=lambda step: -hops(*step))
+
+
+FAR_LON = farthest_first(8, 4, lambda i, j: min(i, 8 - i) + 2 * min(j, 4 - j))
+FAR_GROUP = farthest_first(4, 8, lambda i, j: min(j, 8 - j) + (i > 0))
 
 
 def halves(table):
@@ -104,22 +113,23 @@
     mem, lat, lon = lax.axis_index("mem"), lax.axis_index("lat"), lax.axis_index("lon")
     group = mem * N_LAT + lat
 
+    depth, side = lon // 4, lax.rem(lon, 4)
+
     def lon_peer(d):
-        return {"mem": mem, "lat": lat, "lon": lax.rem(lon + d, N_LON)}
+        return {"mem": mem, "lat": lat, "lon": lax.rem(depth + d[0], 8) * 4 + lax.rem(side + d[1], 4)}
 
     def group_peer(d):
-        other = lax.rem(group + d, N_MEM * N_LAT)
-        return {"mem": other // N_LAT, "lat": lax.rem(other, N_LAT), "lon": lon}
+        return {"mem": lax.rem(mem + d[0], N_MEM), "lat": lax.rem(lat + d[1], N_LAT), "lon": lon}
 
     def mem_peer(d):
         return {"mem": lax.rem(mem + d, N_MEM), "lat": lat, "lon": lon}
 
     barrier = pltpu.get_barrier_semaphore()
 
-    @pl.loop(1, 32)
-    def _(d):
+    for d in FAR_LON:
+        pl.semaphore_signal(barrier, inc=1, device_id=lon_peer(d), device_id_type=MESH)
+    for d in FAR_GROUP:
         pl.semaphore_signal(barrier, inc=1, device_id=group_peer(d), device_id_type=MESH)
-        pl.semaphore_signal(barrier, inc=1, device_id=lon_peer(d), device_id_type=MESH)
 
     loads = [pltpu.make_async_copy(loads_in[k], loads_ref[k], load_sem.at[k]) for k in range(n_load)]
     for copy in loads:
@@ -128,6 +138,14 @@
     own_members.start()
 
     out_c[...] = jnp.zeros_like(out_c)
+
+    pl.semaphore_wait(barrier, 62)
+
+    for d in (2, 3, 1):
+        peer = mem_peer(d)
+        pltpu.make_async_remote_copy(
+            p_ref.at[:, peer["mem"]], mine.at[mem], send_a, recv_a, device_id=peer, device_id_type=MESH
+        ).start()
 
     for k in range(4):
         loads[k].wait()
@@ -154,13 +172,6 @@
     loads[4].wait()
     message = dot_nt(pack[3], chunks[0]) + dot_nt(pack[4], chunks[1])
 
-    pl.semaphore_wait(barrier, 62)
-
-    for d in (2, 3, 1):
-        peer = mem_peer(d)
-        pltpu.make_async_remote_copy(
-            p_ref.at[:, peer["mem"]], mine.at[mem], send_a, recv_a, device_id=peer, device_id_type=MESH
-        ).start()
     own_members.wait()
     three = mine.at[pl.ds(0, 3)]
     pltpu.make_async_copy(three, three, recv_a).wait()
@@ -169,8 +180,7 @@
         message += dot_nt(pack[piece], jnp.concatenate(chunk, axis=0))
     packed[...] = message.astype(BF16).reshape(N_LON, SLOT, 128)
 
-    @pl.loop(1, 32)
-    def _(d):
+    for d in FAR_LON:
         peer = lon_peer(d)
         pltpu.make_async_remote_copy(
             packed.at[peer["lon"]], got.at[lon], send_b, recv_b, device_id=peer, device_id_type=MESH
@@ -263,8 +273,7 @@
         own = jnp.where(place == k, value, own)
 
     def send_sums(stage, part, sums, peer_of, index):
-        @pl.loop(1, 32)
-        def _(d):
+        for d in (FAR_LON, FAR_GROUP)[stage]:
             pltpu.make_async_remote_copy(
                 part, sums.at[index], send_s.at[stage], recv_s.at[stage], device_id=peer_of(d), device_id_type=MESH
             ).start()
@@ -359,7 +368,7 @@
         out_specs=(vmem, vmem),
         scratch_shapes=scratch,
         compiler_params=pltpu.CompilerParams(
-            collective_id=0, has_side_effects=True, vmem_limit_bytes=62 * 1024 * 1024
+            collective_id=0, has_side_effects=True, vmem_limit_bytes=60 * 1024 * 1024
         ),
     )(jnp.swapaxes(perturbations, 2, 3), *obs, cutoff, *consts)
     return jnp.swapaxes(found, 1, 2), jnp.swapaxes(left, 1, 2)

time: 56.6 us -> 55.3 us (0.977)
  Pallas kernels: 53.6 us -> 52.4 us
    pallas_call x1, Pallas kernels: 53.6 us -> 52.4 us  [body(): pl.pallas_call(kernel, out_shape=(out, out), in_specs=[anywhere] * 5 + [p...]
where the time goes in v2:
time: 55.3 us; the launch traced here: 55.1 us
  Pallas kernels  52.4 us (95%)
  local copies, waits for them, and re-layouts  2.06 us (4%)
  between operations  0.65 us (1%)
    pallas_call x1, Pallas kernels, body(): pl.pallas_call(kernel, out_shape=(out, out), in_specs=[anywhere] * 5 + [p...  52.4 us
    unnamed x4, local copies, waits for them, and re-layouts  2.06 us

profile of v2, /device:TPU:1, one launch (start us, length us, event | category | flops | bytes accessed | tf_op | source)
XLA Modules:
  0.0 55.1 jit_solution(12852032669730422834)
XLA Ops:
  0.6 52.4 %shard_map.167 = (f32[2,3,4,512]{3,2,1,0:T(4,128)}, f32[2,3,4,512]{3,2,1,0:T(4,128)}) custom-call(bf16[2,4,48,96]{3,2,1,0:T(8,128)(2,1)} %bitcast.3, f32[1,2048]{1,0:T(1,128)} %inn_in.1, f32[1,2048]{1,0:T(1,128)} %wt_in.1, s32[1,2048]{1,0:T(1,128)} %cell_in.1, s32[1,2048]{1,0:T(1,128)} %lev_in.1, s32[4]{0:T(128)} %cut_ref.1, ...), custom_call_target="tpu_custom_call" | custom-call | tf_op jit(solution)/shard_map/pallas_call | solution.py:364
  53.0 0.0 copy-start
  53.0 1.4 %copy.20 = f32[2,4,3,512]{3,1,2,0:T(4,128)} copy(f32[2,4,3,512]{3,1,2,0:T(4,128)} %bitcast.5) | data formatting | bytes 98304
  54.5 0.0 copy-done
  54.5 0.6 %copy.21 = f32[2,4,3,512]{3,1,2,0:T(4,128)} copy(f32[2,4,3,512]{3,1,2,0:T(4,128)S(1)} %bitcast.4) | data formatting | bytes 98304
Async XLA Ops:
  53.0 1.4 %copy-start = (f32[2,3,4,512]{3,2,1,0:T(4,128)S(1)}, f32[2,3,4,512]{3,2,1,0:T(4,128)}, u32[]{:S(2)}) copy-start(f32[2,3,4,512]{3,2,1,0:T(4,128)} %get-tuple-element.5) | copy-start | bytes 147460

commit v3 on v2

v3 whole, which is shorter than its diff:
```python
import jax
import jax.numpy as jnp
import ml_dtypes
import numpy as np
from jax import lax
from jax.experimental import pallas as pl
from jax.experimental.pallas import tpu as pltpu
from jax.sharding import PartitionSpec as P

MESH = pl.DeviceIdType.MESH
BF16 = jnp.bfloat16
F32 = jnp.float32
NLON = 1536
KMAX = 256
MEMBERS = 8
N_MEM = 4
N_LAT = 8
N_LON = 32
ROWS = 96
COLS = 48
LINES = 3
QUARTER = NLON // 4


def farthest_first(first, second, hops):
    steps = [(i, j) for i in range(first) for j in range(second) if i or j]
    return sorted(steps, key=lambda step: -hops(*step))


FAR_LON = farthest_first(8, 4, lambda i, j: min(i, 8 - i) + 2 * min(j, 4 - j))
FAR_ALL = sorted(
    [(k, *step) for k in range(4) for step in [(0, 0), *FAR_LON] if k or any(step)],
    key=lambda step: -(min(step[1], 8 - step[1]) + 2 * min(step[2], 4 - step[2]) + (step[0] > 0)),
)
FAR_LAT = (4, 3, 5, 2, 6, 1, 7)


def halves(table):
    high = table.astype(ml_dtypes.bfloat16)
    low = (table - high.astype(np.float64)).astype(ml_dtypes.bfloat16)
    return np.stack([high, low])


def constants():
    piece, source, i = np.meshgrid(np.arange(3), np.arange(8), np.arange(16), indexing="ij")
    column = (48 * source + 16 * piece + i).reshape(-1)

    def table(columns, cosines, sines):
        angle = 2.0 * np.pi / NLON
        cos = np.cos((columns[:, None] * cosines[None] % NLON) * angle)
        sin = np.sin((columns[:, None] * sines[None] % NLON) * angle)
        return np.concatenate([cos, sin], axis=1) / 16.0

    c0, s0 = np.arange(0, 256, 4), np.arange(4, 257, 4)
    c2 = np.arange(2, 256, 4)
    c1 = np.arange(1, 256, 2)
    t0 = table(column, c0, s0)
    t2 = table(column, c2, c2)
    t1 = table(np.concatenate([column, QUARTER + column]), c1, c1)
    wave = np.concatenate([c0, s0, c2, c2, c1, c1])
    natural = np.concatenate([c0, 255 + s0, c2, 255 + c2, c1, 255 + c1])
    order = np.zeros((512, 512))
    order[np.arange(512), natural] = 1

    lines = np.zeros((288, 288))
    fields = np.zeros((2, 288, 2, 96))
    for quarter in range(4):
        for piece in range(3):
            for s in range(LINES):
                for m in range(MEMBERS):
                    row = (quarter * 3 + piece) * 24 + s * 8 + m
                    lines[row, ((m % 2) * 3 + piece) * 48 + (m // 2) * 12 + quarter * 3 + s] = 1
                    for f in range(2):
                        k, q = divmod(3 * f + piece, 2)
                        fields[f, row, :, q * 48 + k * 12 + quarter * 3 + s] = 1
    small = [a.astype(ml_dtypes.bfloat16) for a in (lines, fields.reshape(576, 192))]
    tables = [halves(t) for t in (t0, t2, t1, t0.T, t2.T, t1.T)]
    return small + tables + [order.astype(ml_dtypes.bfloat16), np.broadcast_to(wave, (8, 512)).astype(np.float32)]


def dot(a, b):
    return jnp.dot(a, b, preferred_element_type=F32)


def dot_nt(a, b):
    return lax.dot_general(a, b, (((1,), (1,)), ((), ())), preferred_element_type=F32)


def split(x):
    high = x.astype(BF16)
    return high, (x - high.astype(F32)).astype(BF16)


def dot3(x, table):
    high, low = split(x)
    both = dot(jnp.concatenate([high, low], axis=0), table[0])
    n = x.shape[0]
    return both[:n] + (both[n:] + dot(high, table[1]))


def kernel(p_ref, inn_in, wt_in, cell_in, lev_in, cut_ref, *refs):
    n_const = 10
    loads_in = (inn_in, wt_in, cell_in, lev_in, p_ref) + refs[:n_const]
    sets_ref, *factor_refs = refs[n_const : n_const + 3]
    scratch = refs[n_const + 3 :]
    n_load = n_const + 5
    loads_ref = scratch[:n_load]
    (packed, got, x_ref, g_ref, n_ref, c_ref, out_c, in_c, part1, sums1, part2, sums2, last, sets) = scratch[n_load : n_load + 14]
    load_sem, send_b, recv_b, send_c, recv_c, send_s, recv_s = scratch[n_load + 14 :]
    inn_ref, wt_ref, cell_ref, lev_ref, p_vmem, to_lines, to_fields, t0, t2, t1, b0, b2, b1, order, wave = loads_ref

    mem, lat, lon = lax.axis_index("mem"), lax.axis_index("lat"), lax.axis_index("lon")

    depth, side = lon // 4, lax.rem(lon, 4)

    def lat_peer(d):
        return {"mem": mem, "lat": lax.rem(lat + d, N_LAT), "lon": lon}

    def mem_peer(d):
        return {"mem": lax.rem(mem + d, N_MEM), "lat": lat, "lon": lon}

    def line_peer(d):
        return {
            "mem": lax.rem(mem + d[0], N_MEM),
            "lat": lat,
            "lon": lax.rem(depth + d[1], 8) * 4 + lax.rem(side + d[2], 4),
        }

    barrier = pltpu.get_barrier_semaphore()

    loads = [pltpu.make_async_copy(loads_in[k], loads_ref[k], load_sem.at[k]) for k in range(n_load)]
    for copy in loads[:5]:
        copy.start()
    for d in FAR_ALL:
        pl.semaphore_signal(barrier, inc=1, device_id=line_peer(d), device_id_type=MESH)
    for d in FAR_LAT:
        pl.semaphore_signal(barrier, inc=1, device_id=lat_peer(d), device_id_type=MESH)

    for copy in loads[5:]:
        copy.start()
    out_c[...] = jnp.zeros_like(out_c)

    for k in range(5):
        loads[k].wait()
    cell = cell_ref[...].astype(F32)
    row_of = jnp.floor((cell + 0.5) * (1.0 / COLS))
    col_of = cell - COLS * row_of
    key = row_of + ROWS * lev_ref[...].astype(F32)
    rows = lax.broadcasted_iota(jnp.int32, (4 * ROWS, 1), 0)
    row_hot = jnp.where(rows.astype(F32) == key, 1.0, 0.0).astype(BF16)
    lane_row = lax.broadcasted_iota(jnp.int32, (32, 1), 0)
    share = 2 * mem + jnp.where(lane_row >= 16, 1, 0)
    field = jnp.where(share >= 3, 1, 0) + jnp.where(share >= 6, 1, 0)
    column = (share - 3 * field) * 16 + lane_row - jnp.where(lane_row >= 16, 16, 0)
    hit = column.astype(F32) == col_of
    weight = wt_ref[...]
    scaled_d, scaled_w = split(weight * inn_ref[...]), split(weight)
    blank = jnp.zeros((ROWS, 2048), BF16)
    tile = jnp.zeros((4 * ROWS, 128), F32)
    for h in range(2):
        value = jnp.where(field == 0, scaled_d[h].astype(F32), jnp.where(field == 1, scaled_w[h].astype(F32), 0.0))
        placed = jnp.where(hit, value, 0.0).astype(BF16)
        tile += dot_nt(row_hot, jnp.concatenate([blank, placed], axis=0))
    same = lax.broadcasted_iota(jnp.int32, (ROWS, ROWS), 0) == lax.broadcasted_iota(jnp.int32, (ROWS, ROWS), 1)
    eye = jnp.where(same, 1.0, 0.0).astype(BF16)
    for k in range(N_MEM):
        both = jnp.concatenate([p_vmem[0, k], p_vmem[1, k], jnp.zeros((32, ROWS), BF16)], axis=0)
        message = dot_nt(eye, both) + tile[k * ROWS : (k + 1) * ROWS]
        packed[k] = message.reshape(N_LON, LINES, 1, 128)

    pl.semaphore_wait(barrier, 134)

    place_here = (lax.rem(lon, 8) * 4 + mem) * 4 + lon // 8
    for d in FAR_ALL:
        peer = line_peer(d)
        pltpu.make_async_remote_copy(
            packed.at[peer["mem"], peer["lon"]], got.at[place_here], send_b, recv_b, device_id=peer, device_id_type=MESH
        ).start()

    got[place_here] = packed[mem, lon]
    for copy in loads[5:]:
        copy.wait()
    cutoff = cut_ref[mem].astype(F32)
    scaled = wave[0:1, :] / cutoff
    spectrum = 1.0 / (1.0 + scaled * scaled)
    lots = got.at[pl.ds(0, 127)]
    pltpu.make_async_copy(lots, lots, recv_b).wait()

    lane = lax.broadcasted_iota(jnp.int32, (48, 128), 1)
    blocks = [got[16 * k : 16 * k + 16].reshape(48, 128) for k in range(8)]
    for bit in range(3):
        width = 16 << bit
        low_side = (lane & width) == 0
        for k in range(8):
            if not k & (1 << bit):
                a, b = blocks[k], blocks[k | (1 << bit)]
                blocks[k] = jnp.where(low_side, a, pltpu.roll(b, width, 1))
                blocks[k | (1 << bit)] = jnp.where(low_side, pltpu.roll(a, 128 - width, 1), b)
    x_all = dot(to_lines[...], jnp.concatenate(blocks[:6], axis=0).astype(BF16))
    f_all = dot(to_fields[...], jnp.concatenate(split(jnp.concatenate(blocks[6:], axis=0)), axis=0))
    for t in range(12):
        x_ref[:, t * 128 : t * 128 + 128] = x_all[t * 24 : t * 24 + 24]
        g_ref[:, t * 128 : t * 128 + 128] = f_all[t * 24 : t * 24 + 24]
        n_ref[:, t * 128 : t * 128 + 128] = f_all[288 + t * 24 : 288 + t * 24 + 24]

    def quarters(x):
        return [x[:, k * QUARTER : (k + 1) * QUARTER] for k in range(4)]

    def analyse(field):
        q0, q1, q2, q3 = quarters(x_ref[...] * field)
        even, odd = q0 + q2, q1 + q3
        found = [
            dot3(even + odd, t0),
            dot3(even - odd, t2),
            dot3(jnp.concatenate([q0 - q2, q1 - q3], axis=1), t1),
        ]
        return jnp.concatenate(found, axis=1) * spectrum

    def synthesize(coeffs):
        scaled = coeffs * spectrum
        e0 = dot3(scaled[:, :128], b0)
        e2 = dot3(scaled[:, 128:256], b2)
        o = dot3(scaled[:, 256:], b1)
        oa, ob = o[:, :QUARTER], o[:, QUARTER:]
        plus, minus = e0 + e2, e0 - e2
        line = jnp.concatenate([plus + oa, minus + ob, plus - oa, minus - ob], axis=1)
        seen = (x_ref[...] * line).reshape(LINES, MEMBERS, NLON)
        total = jnp.sum(seen, axis=1, keepdims=True)
        return jnp.broadcast_to(total, (LINES, MEMBERS, NLON)).reshape(LINES * MEMBERS, NLON)

    def send_coeffs(v, coeffs):
        c_ref[...] = coeffs
        for k in range(N_MEM):
            for m in range(2):
                for s in range(LINES):
                    out_c[v, k, m * LINES + s : m * LINES + s + 1, :] = c_ref[s * 8 + 2 * k + m : s * 8 + 2 * k + m + 1, :]
        for d in (2, 3, 1):
            peer = mem_peer(d)
            pltpu.make_async_remote_copy(
                out_c.at[v, peer["mem"]], in_c.at[v, mem], send_c.at[v], recv_c.at[v], device_id=peer, device_id_type=MESH
            ).start()
        in_c[v, mem] = out_c[v, mem]

    def total_of(x):
        return jnp.sum(x, keepdims=True)

    f0 = g_ref[...]
    coeffs = analyse(f0)
    send_coeffs(0, coeffs)
    u0 = synthesize(coeffs)
    f1 = n_ref[...] * u0
    m1, m2 = total_of(f0 * u0), total_of(f1 * u0)
    coeffs = analyse(f1)
    send_coeffs(1, coeffs)
    u1 = synthesize(coeffs)
    f2 = n_ref[...] * u1
    m3, m4 = total_of(f1 * u1), total_of(f2 * u1)

    place = lax.broadcasted_iota(jnp.int32, (1, 128), 1)
    own = jnp.zeros((1, 128), F32)
    for k, value in enumerate((m1, m2, m3, m4)):
        own = jnp.where(place == k, value, own)

    def send_sums(stage, part, sums, peer_of, index):
        for d in (FAR_ALL, FAR_LAT)[stage]:
            pltpu.make_async_remote_copy(
                part, sums.at[index], send_s.at[stage], recv_s.at[stage], device_id=peer_of(d), device_id_type=MESH
            ).start()

    def wait_sums(stage, sums):
        lots = sums.at[pl.ds(0, sums.shape[0] - 1)]
        pltpu.make_async_copy(lots, lots, recv_s.at[stage]).wait()
        return jnp.sum(sums[...], axis=0)

    part1[...] = own
    send_sums(0, part1, sums1, line_peer, mem * N_LON + lon)
    sums1[mem * N_LON + lon] = own
    send_coeffs(2, analyse(f2))
    own = wait_sums(0, sums1)
    part2[...] = own
    send_sums(1, part2, sums2, lat_peer, lat)
    sums2[lat] = own
    three = in_c.at[0, pl.ds(0, 3)]
    for v in range(3):
        pltpu.make_async_copy(three, three, recv_c.at[v]).wait()
    for v in range(3):
        both = dot(jnp.concatenate(split(in_c[v].reshape(32, 512)), axis=0), order[...])
        last[...] = (both[:32] + both[32:]).reshape(N_MEM, 8, 512)
        for m in range(2):
            for s in range(LINES):
                for k in range(N_MEM):
                    sets[v, m, s, k : k + 1, :] = last[k, m * LINES + s : m * LINES + s + 1, :]
    sets_out = pltpu.make_async_copy(sets, sets_ref, load_sem.at[n_load])
    sets_out.start()
    moments = wait_sums(1, sums2)
    m1, m2, m3, m4 = (total_of(jnp.where(place == k, moments, 0.0)) for k in range(4))

    step = m1 / (m1 + m2)
    rest = 1.0 - step
    norm = rest * rest * m1 - 2.0 * step * rest * m2 + step * step * m3
    growth = norm / m1
    a = rest + growth
    curved = a * a * (m1 + m2) - 2.0 * a * step * (m2 + m3) + step * step * (m3 + m4)
    step_next = norm / curved
    factors = (
        step + step_next * a,
        -step_next * step,
        rest - step_next * a,
        -step - step_next * (a - step),
        step_next * step,
    )
    for k, factor in enumerate((*factors[:2], jnp.zeros((1, 1), F32), *factors[2:])):
        factor_refs[k // 3][k % 3 : k % 3 + 1, :] = jnp.broadcast_to(factor, (1, 512))
    sets_out.wait()

    lots = got.at[pl.ds(0, 127)]
    pltpu.make_async_copy(lots, lots, send_b).wait()
    three = in_c.at[0, pl.ds(0, 3)]
    for v in range(3):
        pltpu.make_async_copy(three, three, send_c.at[v]).wait()
    for stage, sums in enumerate((sums1, sums2)):
        lots = sums.at[pl.ds(0, sums.shape[0] - 1)]
        pltpu.make_async_copy(lots, lots, send_s.at[stage]).wait()


def body(perturbations, innovation, obs_weight, obs_cell, obs_level, cutoff):
    consts = [jnp.asarray(c) for c in constants()]
    vmem = pl.BlockSpec(memory_space=pltpu.VMEM)
    anywhere = pl.BlockSpec(memory_space=pl.ANY)
    sets_shape = jax.ShapeDtypeStruct((3, 2, LINES, N_MEM, 2 * KMAX), F32)
    factor_shape = jax.ShapeDtypeStruct((3, 2 * KMAX), F32)
    dma = pltpu.SemaphoreType.DMA
    obs = (innovation, obs_weight, obs_cell, obs_level)
    turned = jnp.swapaxes(perturbations, 2, 3)
    scratch = [pltpu.VMEM(c.shape, c.dtype) for c in (*obs, turned, *consts)] + [
        pltpu.VMEM((N_MEM, N_LON, LINES, 1, 128), F32),
        pltpu.VMEM((N_MEM * N_LON, LINES, 1, 128), F32),
        pltpu.VMEM((24, NLON), F32),
        pltpu.VMEM((24, NLON), F32),
        pltpu.VMEM((24, NLON), F32),
        pltpu.VMEM((24, 512), F32),
        pltpu.VMEM((3, 4, 8, 512), F32),
        pltpu.VMEM((3, 4, 8, 512), F32),
        pltpu.VMEM((1, 128), F32),
        pltpu.VMEM((N_MEM * N_LON, 1, 128), F32),
        pltpu.VMEM((1, 128), F32),
        pltpu.VMEM((N_LAT, 1, 128), F32),
        pltpu.VMEM((N_MEM, 8, 512), F32),
        pltpu.VMEM((3, 2, LINES, N_MEM, 512), F32),
        dma((len(obs) + 1 + len(consts) + 1,)),
        dma,
        dma,
        dma((3,)),
        dma((3,)),
        dma((2,)),
        dma((2,)),
    ]
    sets, *f = pl.pallas_call(
        kernel,
        out_shape=(sets_shape,) + (factor_shape,) * 2,
        in_specs=[anywhere] * 5 + [pl.BlockSpec(memory_space=pltpu.SMEM)] + [anywhere] * len(consts),
        out_specs=(anywhere,) + (vmem,) * 2,
        scratch_shapes=scratch,
        compiler_params=pltpu.CompilerParams(
            collective_id=0, has_side_effects=True, vmem_limit_bytes=60 * 1024 * 1024
        ),
    )(turned, *obs, cutoff, *consts)
    found, left = (jnp.sum(factor[:, None, None, None] * sets, axis=0) for factor in f)
    return jnp.swapaxes(found, 1, 2), jnp.swapaxes(left, 1, 2)


def solution(mesh):
    in_specs = (
        P("mem", None, "lat", "lon"),
        P("lat", "lon"),
        P("lat", "lon"),
        P("lat", "lon"),
        P("lat", "lon"),
        P(),
    )
    out_specs = (P("mem", None, ("lat", "lon"), None), P("mem", None, ("lat", "lon"), None))
    return jax.shard_map(body, mesh=mesh, in_specs=in_specs, out_specs=out_specs, check_vma=False)
```

time: 55.3 us -> 52.1 us (0.942)
  Pallas kernels: 52.4 us -> 49.6 us
  local copies, waits for them, and re-layouts: 2.06 us -> 0 us
  other arithmetic: 0 us -> 1.65 us
    pallas_call x1, Pallas kernels: 52.4 us -> 49.6 us  [body(): pl.pallas_call(kernel, out_shape=(sets_shape,) + (factor_shape,) * 2, in_...]
    unnamed x4 -> x0, local copies, waits for them, and re-layouts: 2.06 us -> none
    reduce_sum x0 -> x1, other arithmetic: none -> 1.65 us  [body(): jnp.sum(factor[:, None, None, None] * sets, axis=0)]
where the time goes in v3:
time: 52.1 us; the launch traced here: 51.9 us
  Pallas kernels  49.6 us (95%)
  other arithmetic  1.65 us (3%)
  between operations  0.64 us (1%)
    pallas_call x1, Pallas kernels, body(): pl.pallas_call(kernel, out_shape=(sets_shape,) + (factor_shape,) * 2, in_...  49.6 us
    reduce_sum x1, other arithmetic, body(): jnp.sum(factor[:, None, None, None] * sets, axis=0)  1.65 us

profile of v3, /device:TPU:1, one launch (start us, length us, event | category | flops | bytes accessed | tf_op | source)
XLA Modules:
  0.0 51.9 jit_solution(9934705556173280824)
XLA Ops:
  0.6 49.6 %shard_map.167 = (f32[3,2,3,4,512]{4,3,2,1,0:T(4,128)}, f32[3,512]{1,0:T(4,128)}, f32[3,512]{1,0:T(4,128)}) custom-call(bf16[2,4,48,96]{3,2,1,0:T(8,128)(2,1)} %bitcast.3, f32[1,2048]{1,0:T(1,128)} %inn_in.1, f32[1,2048]{1,0:T(1,128)} %wt_in.1, s32[1,2048]{1,0:T(1,128)} %cell_in.1, s32[1,2048]{1,0:T(1,128)} %lev_in.1, s32[4]{0:T(128)} %cut_ref.1, ...), custom_call_target="tpu_custom_call" | custom-call | tf_op jit(solution)/shard_map/pallas_call | solution.py:358
  50.2 1.7 %multiply_reduce_fusion = (f32[2,3,4,512]{3,2,1,0:T(4,128)}, f32[2,3,4,512]{3,2,1,0:T(4,128)}) fusion(f32[3,2,3,4,512]{4,3,2,1,0:T(4,128)} %get-tuple-element.6, f32[3,512]{1,0:T(4,128)} %get-tuple-element.7, f32[3,512]{1,0:T(4,128)} %get-tuple-element.5), kind=kLoop, calls=%fused_computation | loop fusion | flops 122880 | bytes 258048 | tf_op jit(solution)/shard_map/reduce_sum | solution.py:368

commit v4 on v3

--- a/solution.py
+++ b/solution.py
@@ -32,7 +32,7 @@
     [(k, *step) for k in range(4) for step in [(0, 0), *FAR_LON] if k or any(step)],
     key=lambda step: -(min(step[1], 8 - step[1]) + 2 * min(step[2], 4 - step[2]) + (step[0] > 0)),
 )
-FAR_LAT = (4, 3, 5, 2, 6, 1, 7)
+FAR_GROUP = farthest_first(4, 8, lambda i, j: min(j, 8 - j) + (i > 0))
 
 
 def halves(table):
@@ -98,23 +98,27 @@
     return both[:n] + (both[n:] + dot(high, table[1]))
 
 
-def kernel(p_ref, inn_in, wt_in, cell_in, lev_in, cut_ref, *refs):
+def kernel(p_ref, inn_in, wt_in, cell_in, lev_in, cut_in, *refs):
     n_const = 10
-    loads_in = (inn_in, wt_in, cell_in, lev_in, p_ref) + refs[:n_const]
+    loads_in = (inn_in, wt_in, cell_in, lev_in, p_ref, cut_in) + refs[:n_const]
     sets_ref, *factor_refs = refs[n_const : n_const + 3]
     scratch = refs[n_const + 3 :]
-    n_load = n_const + 5
+    n_load = n_const + 6
     loads_ref = scratch[:n_load]
     (packed, got, x_ref, g_ref, n_ref, c_ref, out_c, in_c, part1, sums1, part2, sums2, last, sets) = scratch[n_load : n_load + 14]
     load_sem, send_b, recv_b, send_c, recv_c, send_s, recv_s = scratch[n_load + 14 :]
-    inn_ref, wt_ref, cell_ref, lev_ref, p_vmem, to_lines, to_fields, t0, t2, t1, b0, b2, b1, order, wave = loads_ref
+    inn_ref, wt_ref, cell_ref, lev_ref, p_vmem, cut_ref, to_lines, to_fields, t0, t2, t1, b0, b2, b1, order, wave = loads_ref
 
     mem, lat, lon = lax.axis_index("mem"), lax.axis_index("lat"), lax.axis_index("lon")
 
+    group = mem * N_LAT + lat
     depth, side = lon // 4, lax.rem(lon, 4)
 
-    def lat_peer(d):
-        return {"mem": mem, "lat": lax.rem(lat + d, N_LAT), "lon": lon}
+    def lon_peer(d):
+        return line_peer((0, *d))
+
+    def group_peer(d):
+        return {"mem": lax.rem(mem + d[0], N_MEM), "lat": lax.rem(lat + d[1], N_LAT), "lon": lon}
 
     def mem_peer(d):
         return {"mem": lax.rem(mem + d, N_MEM), "lat": lat, "lon": lon}
@@ -129,12 +133,15 @@
     barrier = pltpu.get_barrier_semaphore()
 
     loads = [pltpu.make_async_copy(loads_in[k], loads_ref[k], load_sem.at[k]) for k in range(n_load)]
+    for d in FAR_ALL[:64]:
+        pl.semaphore_signal(barrier, inc=1, device_id=line_peer(d), device_id_type=MESH)
     for copy in loads[:5]:
         copy.start()
-    for d in FAR_ALL:
+    for d in FAR_ALL[64:]:
         pl.semaphore_signal(barrier, inc=1, device_id=line_peer(d), device_id_type=MESH)
-    for d in FAR_LAT:
-        pl.semaphore_signal(barrier, inc=1, device_id=lat_peer(d), device_id_type=MESH)
+    for d in FAR_GROUP:
+        if d[1]:
+            pl.semaphore_signal(barrier, inc=1, device_id=group_peer(d), device_id_type=MESH)
 
     for copy in loads[5:]:
         copy.start()
@@ -168,7 +175,7 @@
         message = dot_nt(eye, both) + tile[k * ROWS : (k + 1) * ROWS]
         packed[k] = message.reshape(N_LON, LINES, 1, 128)
 
-    pl.semaphore_wait(barrier, 134)
+    pl.semaphore_wait(barrier, 155)
 
     place_here = (lax.rem(lon, 8) * 4 + mem) * 4 + lon // 8
     for d in FAR_ALL:
@@ -180,7 +187,8 @@
     got[place_here] = packed[mem, lon]
     for copy in loads[5:]:
         copy.wait()
-    cutoff = cut_ref[mem].astype(F32)
+    this_level = lax.broadcasted_iota(jnp.int32, (1, N_MEM), 1) == mem
+    cutoff = jnp.sum(jnp.where(this_level, cut_ref[...].astype(F32), 0.0), keepdims=True)
     scaled = wave[0:1, :] / cutoff
     spectrum = 1.0 / (1.0 + scaled * scaled)
     lots = got.at[pl.ds(0, 127)]
@@ -262,7 +270,7 @@
         own = jnp.where(place == k, value, own)
 
     def send_sums(stage, part, sums, peer_of, index):
-        for d in (FAR_ALL, FAR_LAT)[stage]:
+        for d in (FAR_GROUP, FAR_LON)[stage]:
             pltpu.make_async_remote_copy(
                 part, sums.at[index], send_s.at[stage], recv_s.at[stage], device_id=peer_of(d), device_id_type=MESH
             ).start()
@@ -273,13 +281,13 @@
         return jnp.sum(sums[...], axis=0)
 
     part1[...] = own
-    send_sums(0, part1, sums1, line_peer, mem * N_LON + lon)
-    sums1[mem * N_LON + lon] = own
+    send_sums(0, part1, sums1, group_peer, group)
+    sums1[group] = own
     send_coeffs(2, analyse(f2))
     own = wait_sums(0, sums1)
     part2[...] = own
-    send_sums(1, part2, sums2, lat_peer, lat)
-    sums2[lat] = own
+    send_sums(1, part2, sums2, lon_peer, lon)
+    sums2[lon] = own
     three = in_c.at[0, pl.ds(0, 3)]
     for v in range(3):
         pltpu.make_async_copy(three, three, recv_c.at[v]).wait()
@@ -332,7 +340,8 @@
     dma = pltpu.SemaphoreType.DMA
     obs = (innovation, obs_weight, obs_cell, obs_level)
     turned = jnp.swapaxes(perturbations, 2, 3)
-    scratch = [pltpu.VMEM(c.shape, c.dtype) for c in (*obs, turned, *consts)] + [
+    limits = cutoff.reshape(1, N_MEM)
+    scratch = [pltpu.VMEM(c.shape, c.dtype) for c in (*obs, turned, limits, *consts)] + [
         pltpu.VMEM((N_MEM, N_LON, LINES, 1, 128), F32),
         pltpu.VMEM((N_MEM * N_LON, LINES, 1, 128), F32),
         pltpu.VMEM((24, NLON), F32),
@@ -342,12 +351,12 @@
         pltpu.VMEM((3, 4, 8, 512), F32),
         pltpu.VMEM((3, 4, 8, 512), F32),
         pltpu.VMEM((1, 128), F32),
-        pltpu.VMEM((N_MEM * N_LON, 1, 128), F32),
+        pltpu.VMEM((N_LON, 1, 128), F32),
         pltpu.VMEM((1, 128), F32),
-        pltpu.VMEM((N_LAT, 1, 128), F32),
+        pltpu.VMEM((N_MEM * N_LAT, 1, 128), F32),
         pltpu.VMEM((N_MEM, 8, 512), F32),
         pltpu.VMEM((3, 2, LINES, N_MEM, 512), F32),
-        dma((len(obs) + 1 + len(consts) + 1,)),
+        dma((len(obs) + 2 + len(consts) + 1,)),
         dma,
         dma,
         dma((3,)),
@@ -358,13 +367,13 @@
     sets, *f = pl.pallas_call(
         kernel,
         out_shape=(sets_shape,) + (factor_shape,) * 2,
-        in_specs=[anywhere] * 5 + [pl.BlockSpec(memory_space=pltpu.SMEM)] + [anywhere] * len(consts),
+        in_specs=[anywhere] * (6 + len(consts)),
         out_specs=(anywhere,) + (vmem,) * 2,
         scratch_shapes=scratch,
         compiler_params=pltpu.CompilerParams(
             collective_id=0, has_side_effects=True, vmem_limit_bytes=60 * 1024 * 1024
         ),
-    )(turned, *obs, cutoff, *consts)
+    )(turned, *obs, limits, *consts)
     found, left = (jnp.sum(factor[:, None, None, None] * sets, axis=0) for factor in f)
     return jnp.swapaxes(found, 1, 2), jnp.swapaxes(left, 1, 2)
 

time: 52.1 us -> 51.3 us (0.985)
  Pallas kernels: 49.6 us -> 48.8 us
    pallas_call x1, Pallas kernels: 49.6 us -> 48.8 us  [body(): pl.pallas_call(kernel, out_shape=(sets_shape,) + (factor_shape,) * 2, in_...]
where the time goes in v4:
time: 51.3 us; the launch traced here: 51.1 us
  Pallas kernels  48.8 us (95%)
  other arithmetic  1.65 us (3%)
  between operations  0.64 us (1%)
    pallas_call x1, Pallas kernels, body(): pl.pallas_call(kernel, out_shape=(sets_shape,) + (factor_shape,) * 2, in_...  48.8 us
    reduce_sum x1, other arithmetic, body(): jnp.sum(factor[:, None, None, None] * sets, axis=0)  1.65 us

profile of v4, /device:TPU:1, one launch (start us, length us, event | category | flops | bytes accessed | tf_op | source)
XLA Modules:
  0.0 51.1 jit_solution(17318678515597542764)
XLA Ops:
  0.6 48.8 %shard_map.167 = (f32[3,2,3,4,512]{4,3,2,1,0:T(4,128)}, f32[3,512]{1,0:T(4,128)}, f32[3,512]{1,0:T(4,128)}) custom-call(bf16[2,4,48,96]{3,2,1,0:T(8,128)(2,1)} %bitcast.4, f32[1,2048]{1,0:T(1,128)} %inn_in.1, f32[1,2048]{1,0:T(1,128)} %wt_in.1, s32[1,2048]{1,0:T(1,128)} %cell_in.1, s32[1,2048]{1,0:T(1,128)} %lev_in.1, s32[1,4]{1,0:T(1,128)} %bitcast.7, ...), custom_call_target="tpu_custom_call" | custom-call | tf_op jit(solution)/shard_map/pallas_call | solution.py:367
  49.5 1.7 %multiply_reduce_fusion = (f32[2,3,4,512]{3,2,1,0:T(4,128)}, f32[2,3,4,512]{3,2,1,0:T(4,128)}) fusion(f32[3,2,3,4,512]{4,3,2,1,0:T(4,128)} %get-tuple-element.6, f32[3,512]{1,0:T(4,128)} %get-tuple-element.7, f32[3,512]{1,0:T(4,128)} %get-tuple-element.5), kind=kLoop, calls=%fused_computation | loop fusion | flops 122880 | bytes 258048 | tf_op jit(solution)/shard_map/reduce_sum | solution.py:377

commit v5 on v4

--- a/solution.py
+++ b/solution.py
@@ -253,14 +253,12 @@
         return jnp.sum(x, keepdims=True)
 
     f0 = g_ref[...]
-    coeffs = analyse(f0)
-    send_coeffs(0, coeffs)
-    u0 = synthesize(coeffs)
+    coeffs0 = analyse(f0)
+    u0 = synthesize(coeffs0)
     f1 = n_ref[...] * u0
     m1, m2 = total_of(f0 * u0), total_of(f1 * u0)
-    coeffs = analyse(f1)
-    send_coeffs(1, coeffs)
-    u1 = synthesize(coeffs)
+    coeffs1 = analyse(f1)
+    u1 = synthesize(coeffs1)
     f2 = n_ref[...] * u1
     m3, m4 = total_of(f1 * u1), total_of(f2 * u1)
 
@@ -283,6 +281,8 @@
     part1[...] = own
     send_sums(0, part1, sums1, group_peer, group)
     sums1[group] = own
+    send_coeffs(0, coeffs0)
+    send_coeffs(1, coeffs1)
     send_coeffs(2, analyse(f2))
     own = wait_sums(0, sums1)
     part2[...] = own

time: 51.3 us -> 51 us (level)
  no operation moved by 1% of the time
where the time goes in v5:
time: 51 us; the launch traced here: 50.8 us
  Pallas kernels  48.5 us (95%)
  other arithmetic  1.65 us (3%)
  between operations  0.64 us (1%)
    pallas_call x1, Pallas kernels, body(): pl.pallas_call(kernel, out_shape=(sets_shape,) + (factor_shape,) * 2, in_...  48.5 us
    reduce_sum x1, other arithmetic, body(): jnp.sum(factor[:, None, None, None] * sets, axis=0)  1.65 us

profile of v5, /device:TPU:1, one launch (start us, length us, event | category | flops | bytes accessed | tf_op | source)
XLA Modules:
  0.0 50.8 jit_solution(4773889772183617342)
XLA Ops:
  0.6 48.5 %shard_map.167 = (f32[3,2,3,4,512]{4,3,2,1,0:T(4,128)}, f32[3,512]{1,0:T(4,128)}, f32[3,512]{1,0:T(4,128)}) custom-call(bf16[2,4,48,96]{3,2,1,0:T(8,128)(2,1)} %bitcast.4, f32[1,2048]{1,0:T(1,128)} %inn_in.1, f32[1,2048]{1,0:T(1,128)} %wt_in.1, s32[1,2048]{1,0:T(1,128)} %cell_in.1, s32[1,2048]{1,0:T(1,128)} %lev_in.1, s32[1,4]{1,0:T(1,128)} %bitcast.7, ...), custom_call_target="tpu_custom_call" | custom-call | tf_op jit(solution)/shard_map/pallas_call | solution.py:367
  49.2 1.7 %multiply_reduce_fusion = (f32[2,3,4,512]{3,2,1,0:T(4,128)}, f32[2,3,4,512]{3,2,1,0:T(4,128)}) fusion(f32[3,2,3,4,512]{4,3,2,1,0:T(4,128)} %get-tuple-element.6, f32[3,512]{1,0:T(4,128)} %get-tuple-element.7, f32[3,512]{1,0:T(4,128)} %get-tuple-element.5), kind=kLoop, calls=%fused_computation | loop fusion | flops 122880 | bytes 258048 | tf_op jit(solution)/shard_map/reduce_sum | solution.py:377
